TPU v7x, 32 devices: a whole 2x2x4 slice. The times are simulated.
32 devices in a mesh: groups: 2 (over y), row: 2 (over x), col: 4 (over z), depth: 2 (over core).
Axes of the slice: x: 2, y: 2, z: 4, core: 2. Of those that a mesh axis runs over, the one named last changes fastest.
Arguments:
- layer_input: bfloat16 [4, 224, 4096], P(('groups', 'depth'), 'row', 'col'), parts along dimension 0, may hold values from -6 to 6
- out_grad: bfloat16 [4, 224, 4096], P(('groups', 'depth'), 'row', 'col'), parts along dimension 0, may hold values from -6 to 6
- gate_pre: bfloat16 [4, 224, 14336], P(('groups', 'depth'), 'col', 'row'), parts along dimension 0, may hold values from -6 to 6
- up_pre: bfloat16 [4, 224, 14336], P(('groups', 'depth'), 'col', 'row'), parts along dimension 0, may hold values from -6 to 6
- gate_weight: bfloat16 [4096, 14336], P('col', ('row', 'depth')), may hold values from -0.09375 to 0.09375
- up_weight: bfloat16 [4096, 14336], P('col', ('row', 'depth')), may hold values from -0.09375 to 0.09375
- down_weight: bfloat16 [14336, 4096], P(('row', 'depth'), 'col'), may hold values from -0.046875 to 0.046875
Outputs:
- input_grad: bfloat16 [4, 224, 4096], P(('groups', 'depth'), 'row', 'col'), parts along dimension 0
- gate_weight_grad: bfloat16 [4, 4096, 14336], P(('groups', 'depth'), 'col', 'row'), parts along dimension 0
- up_weight_grad: bfloat16 [4, 4096, 14336], P(('groups', 'depth'), 'col', 'row'), parts along dimension 0
- down_weight_grad: bfloat16 [4, 14336, 4096], P(('groups', 'depth'), 'row', 'col'), parts along dimension 0
There are 2 independent parts, one for each index of `groups`. A program takes and returns all parts, laid end to end along the dimension named above; an argument that names none is the same for every part. Nothing has to cross between parts.
All inputs are finite; a program needn't handle non-finite values.
Results may differ from a plain program's by a relative error of at most 0.03.
Values may be sent and summed in bfloat16 or wider, within the bound.
A program may use at most 192 MiB of HBM per device.

v0:
```python
import jax
import jax.numpy as jnp
from jax import lax
from jax.sharding import PartitionSpec as P


def swiglu_grads(hidden_grad, gate_rows, up_rows):
    gate_value = gate_rows.astype(jnp.float32)
    up_value = up_rows.astype(jnp.float32)
    sig = jax.nn.sigmoid(gate_value)
    silu_value = gate_value * sig
    hidden = (silu_value * up_value).astype(jnp.bfloat16)
    gate_grad = (hidden_grad * up_value * sig * (1.0 + gate_value * (1.0 - sig))).astype(
        jnp.bfloat16
    )
    up_grad = (hidden_grad * silu_value).astype(jnp.bfloat16)
    return (gate_grad, up_grad, hidden)


def times_transposed(left, right):
    return lax.dot_general(
        left, right, (((1,), (1,)), ((), ())), preferred_element_type=jnp.float32
    )


def over_tokens(left, right):
    return lax.dot_general(
        left, right, (((0,), (0,)), ((), ())), preferred_element_type=jnp.float32
    )


def shards(layer_input, out_grad, gate_pre, up_pre, gate_weight, up_weight, down_weight):
    gate_full, up_full, down_full = (
        lax.all_gather(gate_weight, "depth", axis=1, tiled=True),
        lax.all_gather(up_weight, "depth", axis=1, tiled=True),
        lax.all_gather(down_weight, "depth", axis=0, tiled=True),
    )
    input_rows, grad_rows = (
        lax.all_gather(layer_input[0], "row", axis=0, tiled=True),
        lax.all_gather(out_grad[0], "row", axis=0, tiled=True),
    )
    gate_rows, up_rows = (
        lax.all_gather(gate_pre[0], "col", axis=0, tiled=True),
        lax.all_gather(up_pre[0], "col", axis=0, tiled=True),
    )
    partial_hidden = times_transposed(grad_rows, down_full)
    hidden_grad = lax.psum(partial_hidden.astype(jnp.bfloat16), "col").astype(jnp.float32)
    gate_grad, up_grad, hidden = swiglu_grads(hidden_grad, gate_rows, up_rows)
    gate_wgrad = over_tokens(input_rows, gate_grad).astype(jnp.bfloat16)
    up_wgrad = over_tokens(input_rows, up_grad).astype(jnp.bfloat16)
    down_wgrad = over_tokens(hidden, grad_rows).astype(jnp.bfloat16)
    input_share = lax.psum_scatter(
        (times_transposed(gate_grad, gate_full) + times_transposed(up_grad, up_full)).astype(
            jnp.bfloat16
        ),
        "row",
        scatter_dimension=0,
        tiled=True,
    )
    return (input_share[None], gate_wgrad[None], up_wgrad[None], down_wgrad[None])


def solution(mesh):
    return jax.shard_map(
        shards,
        mesh=mesh,
        in_specs=(
            P(("groups", "depth"), "row", "col"),
            P(("groups", "depth"), "row", "col"),
            P(("groups", "depth"), "col", "row"),
            P(("groups", "depth"), "col", "row"),
            P("col", ("row", "depth")),
            P("col", ("row", "depth")),
            P(("row", "depth"), "col"),
        ),
        out_specs=(
            P(("groups", "depth"), "row", "col"),
            P(("groups", "depth"), "col", "row"),
            P(("groups", "depth"), "col", "row"),
            P(("groups", "depth"), "row", "col"),
        ),
        check_vma=False,
    )
```

profile of v0, /device:TPU:0, one launch (start us, length us, event | category | flops | bytes accessed | tf_op | source)
XLA Modules:
  0.0 433.5 jit_solution(16787232423276558372)
XLA Ops:
  7.2 0.0 copy-start.1
  7.2 0.0 all-gather.10.cloned.1.call-start
  7.2 0.7 all-gather.10.cloned.1.call-update
  7.9 0.0 all-gather.18.cloned.1.call-start
  8.0 0.7 all-gather.18.cloned.1.call-update
  8.7 0.0 all-gather.16.cloned.1.call-start
  8.7 0.7 all-gather.16.cloned.1.call-update
  9.4 0.0 all-reduce.2.cloned.1.call-start
  9.4 0.0 copy-done.1
  9.4 9.2 %all-gather = bf16[1,224,1024]{2,1,0:T(8,128)(2,1)S(1)} all-gather(bf16[1,112,1024]{2,1,0:T(8,128)(2,1)S(1)} %copy-done.1), channel_id=2, replica_groups=mesh['groups'=2,'row'=2,'col'=4,'depth'=2] {'row'}, dimensions={1}, use_global_device_ids=true | all-gather | bytes 688128 | tf_op jit(solution)/shard_map/all_gather | solution.py:40
  18.7 20.7 %all-gather.10.cloned.1.call-done = bf16[7168,1024]{1,0:T(8,128)(2,1)} async-done(((bf16[3584,1024]{1,0:T(8,128)(2,1)}), bf16[7168,1024]{1,0:T(8,128)(2,1)}) %all-gather.10.cloned.1.call-update) | async-done | bytes 14680080 | tf_op jit(solution)/shard_map/all_gather | solution.py:36
  39.3 15.9 %convolution_convert_fusion = bf16[224,7168]{1,0:T(8,128)(2,1)} fusion(bf16[7168,1024]{1,0:T(8,128)(2,1)} %all-gather.10.cloned.1.call-done, bf16[1,224,1024]{2,1,0:T(8,128)(2,1)S(1)} %all-gather), kind=kOutput, calls=%fused_computation.6 | convolution fusion | flops 3289939968 | bytes 18350080 | tf_op jit(solution)/shard_map/dot_general | solution.py:21
  55.3 0.0 all-reduce.2.cloned.1.call-update
  55.3 0.0 copy-start.2
  55.3 0.0 all-gather.12.cloned.1.call-start
  55.4 0.5 all-gather.12.cloned.1.call-update
  55.9 0.0 all-gather.14.cloned.1.call-start
  56.0 0.5 all-gather.14.cloned.1.call-update
  56.5 0.0 reduce-scatter.2.cloned.1.call-start
  56.5 0.0 copy-done.2
  56.5 8.7 %all-gather.3 = bf16[1,224,1024]{2,1,0:T(8,128)(2,1)} all-gather(bf16[1,112,1024]{2,1,0:T(8,128)(2,1)S(1)} %copy-done.2), channel_id=5, replica_groups=mesh['groups'=2,'row'=2,'col'=4,'depth'=2] {'row'}, dimensions={1}, use_global_device_ids=true | all-gather | bytes 688128 | tf_op jit(solution)/shard_map/all_gather | solution.py:39
  65.3 41.4 %all-gather.18.cloned.1.call-done = bf16[1,224,7168]{2,1,0:T(8,128)(2,1)} async-done(((bf16[1,56,7168]{2,1,0:T(8,128)(2,1)}), bf16[1,224,7168]{2,1,0:T(8,128)(2,1)}) %all-gather.18.cloned.1.call-update) | async-done | bytes 3211280 | tf_op jit(solution)/shard_map/all_gather | solution.py:43
  106.7 64.8 %all-gather.16.cloned.1.call-done = bf16[1,224,7168]{2,1,0:T(8,128)(2,1)} async-done(((bf16[1,56,7168]{2,1,0:T(8,128)(2,1)}), bf16[1,224,7168]{2,1,0:T(8,128)(2,1)}) %all-gather.16.cloned.1.call-update) | async-done | bytes 3211280 | tf_op jit(solution)/shard_map/all_gather | solution.py:44
  171.5 10.8 %convert_bitcast_fusion = bf16[1,7168,1024]{2,1,0:T(8,128)(2,1)} fusion(bf16[1,224,7168]{2,1,0:T(8,128)(2,1)} %all-gather.16.cloned.1.call-done, bf16[1,224,7168]{2,1,0:T(8,128)(2,1)} %all-gather.18.cloned.1.call-done, bf16[1,224,1024]{2,1,0:T(8,128)(2,1)S(1)} %all-gather), kind=kOutput, calls=%fused_computation | convolution fusion | flops 3308519424 | bytes 21561344 | tf_op jit(solution)/shard_map/dot_general | solution.py:27
  182.3 113.9 %all-reduce.2.cloned.1.call-done = bf16[224,7168]{1,0:T(8,128)(2,1)} async-done(((bf16[224,7168]{1,0:T(8,128)(2,1)}), bf16[224,7168]{1,0:T(8,128)(2,1)}) %all-reduce.2.cloned.1.call-update) | async-done | bytes 3211280 | tf_op jit(solution)/shard_map/psum | solution.py:47
  296.2 5.3 %fusion.3 = bf16[224,7168]{1,0:T(8,128)(2,1)S(1)} fusion(bf16[224,7168]{1,0:T(8,128)(2,1)} %all-reduce.2.cloned.1.call-done, bf16[1,224,7168]{2,1,0:T(8,128)(2,1)} %all-gather.16.cloned.1.call-done, bf16[1,224,7168]{2,1,0:T(8,128)(2,1)} %all-gather.18.cloned.1.call-done), kind=kLoop, calls=%fused_computation.13 | loop fusion | flops 20873216 | bytes 12845056 | tf_op jit(solution)/shard_map/convert_element_type | solution.py:13
  301.6 22.2 %all-gather.12.cloned.1.call-done = bf16[1024,7168]{1,0:T(8,128)(2,1)} async-done(((bf16[1024,3584]{1,0:T(8,128)(2,1)}), bf16[1024,7168]{1,0:T(8,128)(2,1)}) %all-gather.12.cloned.1.call-update) | async-done | bytes 14680080 | tf_op jit(solution)/shard_map/all_gather | solution.py:34
  323.8 8.7 %fusion.19 = f32[224,1024]{1,0:T(8,128)} fusion(bf16[224,7168]{1,0:T(8,128)(2,1)S(1)} %fusion.3, bf16[1024,7168]{1,0:T(8,128)(2,1)} %all-gather.12.cloned.1.call-done), kind=kOutput, calls=%fused_computation.27 | convolution fusion | flops 3288334336 | bytes 18808832 | tf_op jit(solution)/shard_map/dot_general | solution.py:21
  332.4 21.1 %all-gather.14.cloned.1.call-done = bf16[1024,7168]{1,0:T(8,128)(2,1)} async-done(((bf16[1024,3584]{1,0:T(8,128)(2,1)}), bf16[1024,7168]{1,0:T(8,128)(2,1)}) %all-gather.14.cloned.1.call-update) | async-done | bytes 14680080 | tf_op jit(solution)/shard_map/all_gather | solution.py:35
  353.5 12.8 %fusion.11 = bf16[224,1024]{1,0:T(8,128)(2,1)} fusion(f32[224,1024]{1,0:T(8,128)} %fusion.19, bf16[1024,7168]{1,0:T(8,128)(2,1)} %all-gather.14.cloned.1.call-done, bf16[224,7168]{1,0:T(8,128)(2,1)} %all-reduce.2.cloned.1.call-done, bf16[1,224,7168]{2,1,0:T(8,128)(2,1)} %all-gather.18.cloned.1.call-done), kind=kOutput, calls=%fused_computation.21 | convolution fusion | flops 3301638144 | bytes 22478848 | tf_op jit(solution)/shard_map/dot_general | solution.py:21
  366.3 0.0 reduce-scatter.2.cloned.1.call-update
  366.3 8.6 %convert_bitcast_fusion.2 = bf16[1,1024,7168]{1,2,0:T(8,128)(2,1)} fusion(bf16[224,7168]{1,0:T(8,128)(2,1)S(1)} %fusion.3, bf16[1,224,1024]{2,1,0:T(8,128)(2,1)} %all-gather.3), kind=kOutput, calls=%fused_computation.2 | convolution fusion | flops 3295674368 | bytes 18350080 | tf_op jit(solution)/shard_map/dot_general | solution.py:27
  374.9 0.0 copy-start
  374.9 20.1 %copy.11 = bf16[1,1024,7168]{2,1,0:T(8,128)(2,1)} copy(bf16[1,1024,7168]{1,2,0:T(8,128)(2,1)} %convert_bitcast_fusion.2) | data formatting | bytes 29360128
  395.0 0.0 copy-done
  395.0 11.7 %convert_bitcast_fusion.1 = bf16[1,1024,7168]{1,2,0:T(8,128)(2,1)} fusion(bf16[1,224,1024]{2,1,0:T(8,128)(2,1)} %all-gather.3, bf16[224,7168]{1,0:T(8,128)(2,1)} %all-reduce.2.cloned.1.call-done, bf16[1,224,7168]{2,1,0:T(8,128)(2,1)S(1)} %copy-done), kind=kOutput, calls=%fused_computation.1 | convolution fusion | flops 3308519424 | bytes 21561344 | tf_op jit(solution)/shard_map/dot_general | solution.py:27
  406.7 19.9 %copy.12 = bf16[1,1024,7168]{2,1,0:T(8,128)(2,1)} copy(bf16[1,1024,7168]{1,2,0:T(8,128)(2,1)} %convert_bitcast_fusion.1) | data formatting | bytes 29360128
  426.6 0.0 reduce-scatter.2.cloned.1.call-done
Async XLA Ops:
  7.2 2.3 copy-start.1
  7.2 32.2 %all-gather.10.cloned.1.call-start = ((), (), s32[]{:S(2)}) async-start(), calls=%async_computation.1 | async-start | bytes 22020096 | tf_op jit(solution)/shard_map/all_gather | solution.py:36
  7.9 98.8 %all-gather.18.cloned.1.call-start = ((), (), s32[]{:S(2)}) async-start(), calls=%async_computation.7 | async-start | bytes 4014080 | tf_op jit(solution)/shard_map/all_gather | solution.py:43
  8.7 162.9 %all-gather.16.cloned.1.call-start = ((), (), s32[]{:S(2)}) async-start(), calls=%async_computation.6 | async-start | bytes 4014080 | tf_op jit(solution)/shard_map/all_gather | solution.py:44
  9.4 286.8 %all-reduce.2.cloned.1.call-start = ((), (), s32[]{:S(2)}) async-start(), calls=%async_computation.2 | async-start | bytes 6422528 | tf_op jit(solution)/shard_map/psum | solution.py:47
  55.3 1.2 copy-start.2
  55.3 268.4 %all-gather.12.cloned.1.call-start = ((), (), s32[]{:S(2)}) async-start(), calls=%async_computation.3 | async-start | bytes 22020096 | tf_op jit(solution)/shard_map/all_gather | solution.py:34
  55.9 297.6 %all-gather.14.cloned.1.call-start = ((), (), s32[]{:S(2)}) async-start(), calls=%async_computation.4 | async-start | bytes 22020096 | tf_op jit(solution)/shard_map/all_gather | solution.py:35
  56.5 370.1 %reduce-scatter.2.cloned.1.call-start = ((), (), s32[]{:S(2)}) async-start(), calls=%async_computation.5 | async-start | bytes 688128 | tf_op jit(solution)/shard_map/reduce_scatter | solution.py:52
  374.9 20.1 %copy-start = (bf16[1,224,7168]{2,1,0:T(8,128)(2,1)S(1)}, bf16[1,224,7168]{2,1,0:T(8,128)(2,1)}, u32[]{:S(2)}) copy-start(bf16[1,224,7168]{2,1,0:T(8,128)(2,1)} %all-gather.18.cloned.1.call-done) | copy-start | bytes 9633796
Sparse Core Ops, SparseCore 0:
  9.6 29.7 all-gather.9
  40.9 65.7 all-gather.17
  108.3 63.2 all-gather.15
  174.3 121.8 all-reduce.1
  297.7 26.0 all-gather.11
  325.3 28.1 all-gather.13
  366.4 14.9 reduce-scatter.1
where the time goes:
time: 435 us; the launch traced here: 433 us
  waiting for transfers between devices  287 us (66%)
  matrix products  68.5 us (16%)
  local copies, waits for them, and re-layouts  40 us (9%)
  blocking collectives  17.9 us (4%)
  between operations  14.2 us (3%)
  other arithmetic  5.33 us (1%)
    psum x1, waiting for transfers between devices, shards(): lax.psum(partial_hidden.astype(jnp.bfloat16), 'col').astype(jnp.float32)  114 us
    all_gather x1, waiting for transfers between devices, shards(): lax.all_gather(up_pre[0], 'col', axis=0, tiled=True)  64.8 us
    all_gather x1, waiting for transfers between devices, shards(): lax.all_gather(gate_pre[0], 'col', axis=0, tiled=True)  41.4 us
    unnamed x8, local copies, waits for them, and re-layouts  40 us
    dot_general x3, matrix products, times_transposed(): lax.dot_general(left, right, (((1,), (1,)), ((), ())), preferred_element_...  37.4 us
    dot_general x3, matrix products, over_tokens(): lax.dot_general(left, right, (((0,), (0,)), ((), ())), preferred_element_...  31.2 us
    all_gather x1, waiting for transfers between devices, shards(): lax.all_gather(gate_weight, 'depth', axis=1, tiled=True)  22.2 us
    all_gather x1, waiting for transfers between devices, shards(): lax.all_gather(up_weight, 'depth', axis=1, tiled=True)  21.1 us
  transfers between devices with their start and end apart: 7, of which 6 were waited for; matrix products, arithmetic and copies ran while one was open for 23% of the time, Pallas kernels for 0%

commit v1 on v0

--- a/solution.py
+++ b/solution.py
@@ -2,6 +2,29 @@
 import jax.numpy as jnp
 from jax import lax
 from jax.sharding import PartitionSpec as P
+
+
+def _unite_panel(chunk):
+    local_next, high, x_new = (lax.axis_size("col"), lax.axis_index("col"), chunk.shape[0])
+    items = list(map(lambda ii: (ii, (ii + 1) % local_next), range(local_next)))
+    kept_rows = list(map(lambda ii: (ii, (ii - 1) % local_next), range(local_next)))
+    piece_out = jnp.zeros((*chunk.shape[:0], local_next * x_new, *chunk.shape[1:]), chunk.dtype)
+    piece_out = lax.dynamic_update_slice_in_dim(piece_out, chunk, high * x_new, axis=0)
+    b_now = extra = chunk
+    r_now = local_next // 2
+    hop_no = 1
+    while hop_no < r_now + 1:
+        b_now = lax.ppermute(b_now, "col", items)
+        piece_out = lax.dynamic_update_slice_in_dim(
+            piece_out, b_now, (high - hop_no) % local_next * x_new, axis=0
+        )
+        if hop_no < local_next - r_now:
+            extra = lax.ppermute(extra, "col", kept_rows)
+            piece_out = lax.dynamic_update_slice_in_dim(
+                piece_out, extra, (high + hop_no) % local_next * x_new, axis=0
+            )
+        hop_no = hop_no + 1
+    return piece_out
 
 
 def swiglu_grads(hidden_grad, gate_rows, up_rows):
@@ -41,7 +64,7 @@
     )
     gate_rows, up_rows = (
         lax.all_gather(gate_pre[0], "col", axis=0, tiled=True),
-        lax.all_gather(up_pre[0], "col", axis=0, tiled=True),
+        _unite_panel(up_pre[0]),
     )
     partial_hidden = times_transposed(grad_rows, down_full)
     hidden_grad = lax.psum(partial_hidden.astype(jnp.bfloat16), "col").astype(jnp.float32)

time: 435 us -> 414 us (0.952)
  waiting for transfers between devices: 287 us -> 222 us
  starting transfers between devices: 0.27 us -> 36.6 us
  matrix products: 68.5 us -> 79.4 us
  other arithmetic: 5.33 us -> 0 us
    all_gather x1 -> x0, waiting for transfers between devices: 64.8 us -> none  [shards(): lax.all_gather(up_pre[0], 'col', axis=0, tiled=True)]
    ppermute x0 -> x3, waiting for transfers between devices: none -> 53.4 us  [the longest x2 53.3 us: _unite_panel(): b_now = lax.ppermute(b_now, 'col', items)]
    all_gather x1, waiting for transfers between devices: 41.4 us -> 0.02 us  [shards(): lax.all_gather(gate_pre[0], 'col', axis=0, tiled=True)]
    ppermute x0 -> x3, starting transfers between devices: none -> 36.4 us  [the longest x2 34.3 us: _unite_panel(): b_now = lax.ppermute(b_now, 'col', items)]
    all_gather x1, waiting for transfers between devices: 21.1 us -> 3.34 us  [shards(): lax.all_gather(up_weight, 'depth', axis=1, tiled=True)]
    psum x1, waiting for transfers between devices: 114 us -> 127 us  [shards(): lax.psum(partial_hidden.astype(jnp.bfloat16), 'col').astype(jnp.float32)]
    all_gather x1, waiting for transfers between devices: 22.2 us -> 14.2 us  [shards(): lax.all_gather(gate_weight, 'depth', axis=1, tiled=True)]
    dot_general x3, matrix products: 37.4 us -> 43.2 us  [times_transposed(): lax.dot_general(left, right, (((1,), (1,)), ((), ())), preferred_element_...]
  transfers between devices with their start and end apart: 7 -> 9, of which waited for: 6 -> 7; matrix products, arithmetic and copies ran while one was open for 23% -> 26% of each run, Pallas kernels for 0% -> 0%
where the time goes in v1:
time: 414 us; the launch traced here: 413 us
  waiting for transfers between devices  222 us (54%)
  matrix products  79.4 us (19%)
  local copies, waits for them, and re-layouts  43.9 us (11%)
  starting transfers between devices  36.6 us (9%)
  blocking collectives  17.4 us (4%)
  between operations  14.2 us (3%)
    psum x1, waiting for transfers between devices, shards(): lax.psum(partial_hidden.astype(jnp.bfloat16), 'col').astype(jnp.float32)  127 us
    ppermute x2, waiting for transfers between devices, _unite_panel(): b_now = lax.ppermute(b_now, 'col', items)  53.3 us
    dot_general x3, matrix products, times_transposed(): lax.dot_general(left, right, (((1,), (1,)), ((), ())), preferred_element_...  43.2 us
    unnamed x10, local copies, waits for them, and re-layouts  39.9 us
    dot_general x3, matrix products, over_tokens(): lax.dot_general(left, right, (((0,), (0,)), ((), ())), preferred_element_...  36.2 us
    ppermute x2, starting transfers between devices, _unite_panel(): b_now = lax.ppermute(b_now, 'col', items)  34.3 us
    all_gather x1, waiting for transfers between devices, shards(): lax.all_gather(down_weight, 'depth', axis=0, tiled=True)  20.7 us
    all_gather x1, waiting for transfers between devices, shards(): lax.all_gather(gate_weight, 'depth', axis=1, tiled=True)  14.2 us
  transfers between devices with their start and end apart: 9, of which 7 were waited for; matrix products, arithmetic and copies ran while one was open for 26% of the time, Pallas kernels for 0%

profile of v1, /device:TPU:0, one launch (start us, length us, event | category | flops | bytes accessed | tf_op | source)
XLA Modules:
  0.0 413.0 jit_solution(5712873314332326347)
XLA Ops:
  7.2 0.0 copy-start.2
  7.2 0.0 all-gather.8.cloned.1.call-start
  7.2 0.7 all-gather.8.cloned.1.call-update
  7.9 0.0 all-gather.14.cloned.1.call-start
  8.0 0.7 all-gather.14.cloned.1.call-update
  8.7 0.0 all-gather.12.cloned.1.call-start
  8.7 0.7 all-gather.12.cloned.1.call-update
  9.4 0.0 all-reduce.2.cloned.1.call-start
  9.4 0.0 copy-done.2
  9.4 9.2 %all-gather = bf16[1,224,1024]{2,1,0:T(8,128)(2,1)S(1)} all-gather(bf16[1,112,1024]{2,1,0:T(8,128)(2,1)S(1)} %copy-done.2), channel_id=2, replica_groups=mesh['groups'=2,'row'=2,'col'=4,'depth'=2] {'row'}, dimensions={1}, use_global_device_ids=true | all-gather | bytes 688128 | tf_op jit(solution)/shard_map/all_gather | solution.py:63
  18.7 0.0 copy-start
  18.7 20.7 %all-gather.8.cloned.1.call-done = bf16[7168,1024]{1,0:T(8,128)(2,1)} async-done(((bf16[3584,1024]{1,0:T(8,128)(2,1)}), bf16[7168,1024]{1,0:T(8,128)(2,1)}) %all-gather.8.cloned.1.call-update) | async-done | bytes 14680080 | tf_op jit(solution)/shard_map/all_gather | solution.py:59
  39.3 15.9 %convolution_convert_fusion = bf16[224,7168]{1,0:T(8,128)(2,1)} fusion(bf16[7168,1024]{1,0:T(8,128)(2,1)} %all-gather.8.cloned.1.call-done, bf16[1,224,1024]{2,1,0:T(8,128)(2,1)S(1)} %all-gather), kind=kOutput, calls=%fused_computation.6 | convolution fusion | flops 3289939968 | bytes 18350080 | tf_op jit(solution)/shard_map/dot_general | solution.py:44
  55.3 0.0 copy-done
  55.3 0.0 all-reduce.2.cloned.1.call-update
  55.3 0.0 copy-start.3
  55.3 0.0 all-gather.10.cloned.1.call-start
  55.4 0.5 all-gather.10.cloned.1.call-update
  55.9 0.0 reduce-scatter.2.cloned.1.call-start
  56.0 1.8 collective-permute-start
  57.8 2.1 collective-permute-start.1
  59.8 0.3 broadcast_in_dim.15
  60.2 1.2 constant_dynamic-update-slice_fusion.3
  61.5 0.0 copy-done.3
  61.5 8.1 %all-gather.2 = bf16[1,224,1024]{2,1,0:T(8,128)(2,1)} all-gather(bf16[1,112,1024]{2,1,0:T(8,128)(2,1)S(1)} %copy-done.3), channel_id=4, replica_groups=mesh['groups'=2,'row'=2,'col'=4,'depth'=2] {'row'}, dimensions={1}, use_global_device_ids=true | all-gather | bytes 688128 | tf_op jit(solution)/shard_map/all_gather | solution.py:62
  69.6 26.4 %collective-permute-done = bf16[56,7168]{1,0:T(8,128)(2,1)} collective-permute-done((bf16[56,7168]{1,0:T(8,128)(2,1)}, bf16[56,7168]{1,0:T(8,128)(2,1)}, u32[]{:S(2)}, u32[]{:S(2)}) %collective-permute-start) | collective-permute-done | bytes 802848 | tf_op jit(solution)/shard_map/ppermute | solution.py:17
  96.1 32.5 %collective-permute-start.2 = (bf16[56,7168]{1,0:T(8,128)(2,1)}, bf16[56,7168]{1,0:T(8,128)(2,1)S(1)}, u32[]{:S(2)}, u32[]{:S(2)}) collective-permute-start(bf16[56,7168]{1,0:T(8,128)(2,1)} %collective-permute-done), channel_id=1, source_target_pairs={{0,2},{2,4},{4,6},{6,0},{1,3},{3,5},{5,7},{7,1},{8,10},{10,12},{12... | collective-permute-start | bytes 2408456 | tf_op jit(solution)/shard_map/ppermute | solution.py:17
  128.6 1.2 constant_dynamic-update-slice_fusion.2
  129.8 0.1 collective-permute-done.1
  130.0 1.2 constant_dynamic-update-slice_fusion.1
  131.2 26.9 %collective-permute-done.2 = bf16[56,7168]{1,0:T(8,128)(2,1)S(1)} collective-permute-done((bf16[56,7168]{1,0:T(8,128)(2,1)}, bf16[56,7168]{1,0:T(8,128)(2,1)S(1)}, u32[]{:S(2)}, u32[]{:S(2)}) %collective-permute-start.2) | collective-permute-done | bytes 802848 | tf_op jit(solution)/shard_map/ppermute | solution.py:17
  158.0 0.1 constant_dynamic-update-slice_fusion
  158.1 0.0 all-gather.14.cloned.1.call-done
  158.1 13.6 %convert_bitcast_fusion = bf16[1,7168,1024]{2,1,0:T(8,128)(2,1)} fusion(bf16[224,7168]{1,0:T(8,128)(2,1)S(1)} %constant_dynamic-update-slice_fusion, bf16[1,224,7168]{2,1,0:T(8,128)(2,1)} %all-gather.14.cloned.1.call-done, bf16[1,224,1024]{2,1,0:T(8,128)(2,1)} %copy-done), kind=kOutput, calls=%fused_computation | convolution fusion | flops 3308519424 | bytes 21561344 | tf_op jit(solution)/shard_map/dot_general | solution.py:50
  171.7 3.3 all-gather.12.cloned.1.call-done
  175.1 127.2 %all-reduce.2.cloned.1.call-done = bf16[224,7168]{1,0:T(8,128)(2,1)} async-done(((bf16[224,7168]{1,0:T(8,128)(2,1)}), bf16[224,7168]{1,0:T(8,128)(2,1)}) %all-reduce.2.cloned.1.call-update) | async-done | bytes 3211280 | tf_op jit(solution)/shard_map/psum | solution.py:70
  302.3 13.4 %fusion.17 = f32[224,1024]{1,0:T(8,128)} fusion(bf16[1024,7168]{1,0:T(8,128)(2,1)} %all-gather.12.cloned.1.call-done, bf16[224,7168]{1,0:T(8,128)(2,1)} %all-reduce.2.cloned.1.call-done, bf16[1,224,7168]{2,1,0:T(8,128)(2,1)} %all-gather.14.cloned.1.call-done), kind=kOutput, calls=%fused_computation.30 | convolution fusion | flops 3301179392 | bytes 22020096 | tf_op jit(solution)/shard_map/dot_general | solution.py:44
  315.7 14.2 %all-gather.10.cloned.1.call-done = bf16[1024,7168]{1,0:T(8,128)(2,1)} async-done(((bf16[1024,3584]{1,0:T(8,128)(2,1)}), bf16[1024,7168]{1,0:T(8,128)(2,1)}) %all-gather.10.cloned.1.call-update) | async-done | bytes 14680080 | tf_op jit(solution)/shard_map/all_gather | solution.py:57
  329.9 13.9 %fusion.10 = bf16[224,1024]{1,0:T(8,128)(2,1)} fusion(f32[224,1024]{1,0:T(8,128)} %fusion.17, bf16[1024,7168]{1,0:T(8,128)(2,1)} %all-gather.10.cloned.1.call-done, bf16[224,7168]{1,0:T(8,128)(2,1)S(1)} %constant_dynamic-update-slice_fusion, bf16[224,7168]{1,0:T(8,128)(2,1)} %all-reduce.2.cloned.1.call-done, ...), kind=kOutput, calls=%fused_computation.20 | convolution fusion | flops 3309666304 | bytes 25690112 | tf_op jit(solution)/shard_map/dot_general | solution.py:44
  343.7 0.0 reduce-scatter.2.cloned.1.call-update
  343.8 11.7 %convert_bitcast_fusion.2 = bf16[1,1024,7168]{1,2,0:T(8,128)(2,1)} fusion(bf16[1,224,1024]{2,1,0:T(8,128)(2,1)} %all-gather.2, bf16[224,7168]{1,0:T(8,128)(2,1)S(1)} %constant_dynamic-update-slice_fusion, bf16[224,7168]{1,0:T(8,128)(2,1)} %all-reduce.2.cloned.1.call-done, bf16[1,224,7168]{2,1,0:T(8,128)(2,1)} %all-gather.14.cloned.1.call-done), kind=kOutput, calls=%fused_computation.2 | convolution fusion | flops 3316547584 | bytes 24772608 | tf_op jit(solution)/shard_map/dot_general | solution.py:50
  355.5 0.0 copy-start.1
  355.5 20.0 %copy.11 = bf16[1,1024,7168]{2,1,0:T(8,128)(2,1)} copy(bf16[1,1024,7168]{1,2,0:T(8,128)(2,1)} %convert_bitcast_fusion.2) | data formatting | bytes 29360128
  375.4 0.0 copy-done.1
  375.5 10.8 %convert_bitcast_fusion.1 = bf16[1,1024,7168]{1,2,0:T(8,128)(2,1)} fusion(bf16[1,224,1024]{2,1,0:T(8,128)(2,1)S(1)} %copy-done.1, bf16[224,7168]{1,0:T(8,128)(2,1)} %all-reduce.2.cloned.1.call-done, bf16[1,224,7168]{2,1,0:T(8,128)(2,1)} %all-gather.14.cloned.1.call-done), kind=kOutput, calls=%fused_computation.1 | convolution fusion | flops 3308519424 | bytes 21561344 | tf_op jit(solution)/shard_map/dot_general | solution.py:50
  386.3 19.9 %copy.12 = bf16[1,1024,7168]{2,1,0:T(8,128)(2,1)} copy(bf16[1,1024,7168]{1,2,0:T(8,128)(2,1)} %convert_bitcast_fusion.1) | data formatting | bytes 29360128
  406.2 0.0 reduce-scatter.2.cloned.1.call-done
Async XLA Ops:
  7.2 2.3 copy-start.2
  7.2 32.2 %all-gather.8.cloned.1.call-start = ((), (), s32[]{:S(2)}) async-start(), calls=%async_computation.1 | async-start | bytes 22020096 | tf_op jit(solution)/shard_map/all_gather | solution.py:59
  7.9 150.2 %all-gather.14.cloned.1.call-start = ((), (), s32[]{:S(2)}) async-start(), calls=%async_computation.6 | async-start | bytes 4014080 | tf_op jit(solution)/shard_map/all_gather | solution.py:66
  8.7 166.4 %all-gather.12.cloned.1.call-start = ((), (), s32[]{:S(2)}) async-start(), calls=%async_computation.4 | async-start | bytes 22020096 | tf_op jit(solution)/shard_map/all_gather | solution.py:58
  9.4 292.9 %all-reduce.2.cloned.1.call-start = ((), (), s32[]{:S(2)}) async-start(), calls=%async_computation.2 | async-start | bytes 6422528 | tf_op jit(solution)/shard_map/psum | solution.py:70
  18.7 36.6 %copy-start = (bf16[1,224,1024]{2,1,0:T(8,128)(2,1)}, bf16[1,224,1024]{2,1,0:T(8,128)(2,1)S(1)}, u32[]{:S(2)}) copy-start(bf16[1,224,1024]{2,1,0:T(8,128)(2,1)S(1)} %all-gather) | copy-start | bytes 1376260
  55.3 6.2 %copy-start.3 = (bf16[1,112,1024]{2,1,0:T(8,128)(2,1)S(1)}, bf16[1,112,1024]{2,1,0:T(8,128)(2,1)}, u32[]{:S(2)}) copy-start(bf16[1,112,1024]{2,1,0:T(8,128)(2,1)} %param.7) | copy-start | bytes 688132
  55.3 274.5 %all-gather.10.cloned.1.call-start = ((), (), s32[]{:S(2)}) async-start(), calls=%async_computation.3 | async-start | bytes 22020096 | tf_op jit(solution)/shard_map/all_gather | solution.py:57
  55.9 350.3 %reduce-scatter.2.cloned.1.call-start = ((), (), s32[]{:S(2)}) async-start(), calls=%async_computation.5 | async-start | bytes 688128 | tf_op jit(solution)/shard_map/reduce_scatter | solution.py:75
  56.0 40.1 %collective-permute-start = (bf16[56,7168]{1,0:T(8,128)(2,1)}, bf16[56,7168]{1,0:T(8,128)(2,1)}, u32[]{:S(2)}, u32[]{:S(2)}) collective-permute-start(bf16[56,7168]{1,0:T(8,128)(2,1)} %bitcast.1), channel_id=1, source_target_pairs={{0,2},{2,4},{4,6},{6,0},{1,3},{3,5},{5,7},{7,1},{8,10},{10,12},{12... | collective-permute-start | bytes 2408456 | tf_op jit(solution)/shard_map/ppermute | solution.py:17
  57.8 72.2 %collective-permute-start.1 = (bf16[56,7168]{1,0:T(8,128)(2,1)}, bf16[56,7168]{1,0:T(8,128)(2,1)}, u32[]{:S(2)}, u32[]{:S(2)}) collective-permute-start(bf16[56,7168]{1,0:T(8,128)(2,1)} %bitcast.1), channel_id=1, source_target_pairs={{0,6},{2,0},{4,2},{6,4},{1,7},{3,1},{5,3},{7,5},{8,14},{10,8},{12,... | collective-permute-start | bytes 2408456 | tf_op jit(solution)/shard_map/ppermute | solution.py:22
  96.1 62.0 %collective-permute-start.2 = (bf16[56,7168]{1,0:T(8,128)(2,1)}, bf16[56,7168]{1,0:T(8,128)(2,1)S(1)}, u32[]{:S(2)}, u32[]{:S(2)}) collective-permute-start(bf16[56,7168]{1,0:T(8,128)(2,1)} %collective-permute-done), channel_id=1, source_target_pairs={{0,2},{2,4},{4,6},{6,0},{1,3},{3,5},{5,7},{7,1},{8,10},{10,12},{12... | collective-permute-start | bytes 2408456 | tf_op jit(solution)/shard_map/ppermute | solution.py:17
  355.5 20.0 %copy-start.1 = (bf16[1,224,1024]{2,1,0:T(8,128)(2,1)S(1)}, bf16[1,224,1024]{2,1,0:T(8,128)(2,1)}, u32[]{:S(2)}) copy-start(bf16[1,224,1024]{2,1,0:T(8,128)(2,1)} %all-gather.2) | copy-start | bytes 1376260
Sparse Core Ops, SparseCore 0:
  9.6 29.7 all-gather.7
  40.9 106.3 all-gather.13
  148.9 26.1 all-gather.11
  177.9 124.3 all-reduce.1
  303.8 26.0 all-gather.9
  343.9 14.9 reduce-scatter.1
